TPU v7x, 32 devices: a whole 2x2x4 slice. The times are simulated.
32 devices in a mesh: seq: 4 (over y, x), chan: 8 (over z, core).
Axes of the slice: x: 2, y: 2, z: 4, core: 2. Of those that a mesh axis runs over, the one named last changes fastest.
Arguments:
- hidden: bfloat16 [256, 4096], P('seq', 'chan'), may hold values from -6 to 6
- filters: bfloat16 [256, 4096], P('seq', 'chan'), may hold values from -0.75 to 0.75
- in_weight: bfloat16 [3, 4096, 4096], P(None, None, 'chan'), may hold values from -0.09375 to 0.09375
- out_weight: bfloat16 [4096, 4096], P('chan'), may hold values from -0.125 to 0.125
- block_table: int32 [8], replicated, may hold values from 0 to 7, as said below
Outputs:
- mixed: bfloat16 [256, 4096], P('seq', 'chan')
Inputs may be any that keep to these rules, and one draw needn't show every extreme that they name: `block_table`: each index of seq holds stored blocks 2g and 2g+1, which carry a pair p and 7 - p in either order; every sequence block appears once.
All inputs are finite; a program needn't handle non-finite values.
Results may differ from a plain program's by a relative error of at most 0.0049.
Values may be sent and summed in bfloat16 or wider, within the bound.
A program may use at most 64 MiB of HBM per device.

v0:
```python
import jax
import jax.numpy as jnp
from jax import lax
from jax.sharding import PartitionSpec as P

highest = lax.Precision.HIGHEST


def angle_table(rows, cols, period):
    row_ids = lax.broadcasted_iota(jnp.int32, (rows, cols), 0)
    col_ids = lax.broadcasted_iota(jnp.int32, (rows, cols), 1)
    turns = row_ids * col_ids % period
    return turns.astype(jnp.float32) * (2.0 * jnp.pi / period)


def transform(values, cos_fwd, sin_fwd):
    real_part = jnp.einsum("kt,btc->bkc", cos_fwd, values, precision=highest)
    imag_part = -jnp.einsum("kt,btc->bkc", sin_fwd, values, precision=highest)
    return (real_part, imag_part)


def on_device(hidden, filters, in_weight, out_weight, block_table):
    seg = hidden.shape[0] // 2
    width = 2 * seg
    chans = hidden.shape[1]
    streams = jnp.einsum(
        "tn,snc->stc",
        lax.all_gather(hidden, "chan", axis=1, tiled=True),
        in_weight,
        preferred_element_type=jnp.float32,
    )
    query = streams[0]
    mixed_in = (streams[1] * streams[2]).reshape(2, seg, chans)
    fwd_angle = angle_table(width, seg, width)
    cos_fwd = jnp.cos(fwd_angle)
    sin_fwd = jnp.sin(fwd_angle)
    lags = lax.all_gather(filters, "seq", axis=0, tiled=True).astype(jnp.float32)
    count = lags.shape[0] // seg
    lower = lags.reshape(count, seg, chans)
    earlier = jnp.concatenate([jnp.zeros((1, seg, chans), jnp.float32), lower[:-1]], axis=0)
    segments = jnp.concatenate(
        [lower, jnp.zeros((count, 1, chans), jnp.float32), earlier[:, 1:]], axis=1
    )
    full_angle = angle_table(width, width, width)
    filt_real = jnp.einsum("kt,mtc->mkc", jnp.cos(full_angle), segments, precision=highest)
    filt_imag = -jnp.einsum("kt,mtc->mkc", jnp.sin(full_angle), segments, precision=highest)
    mine = lax.dynamic_slice_in_dim(block_table, lax.axis_index("seq") * 2, 2)
    own_real, own_imag = transform(mixed_in, cos_fwd, sin_fwd)
    piece_real = lax.all_gather(own_real, "seq", axis=0, tiled=True)
    piece_imag = lax.all_gather(own_imag, "seq", axis=0, tiled=True)
    outs_real = []
    outs_imag = []
    for own in range(2):
        lag = mine[own] - block_table
        valid = (lag >= 0).astype(jnp.float32)[:, None, None]
        lag_safe = jnp.clip(lag, 0, count - 1)
        h_real = jnp.take(filt_real, lag_safe, axis=0) * valid
        h_imag = jnp.take(filt_imag, lag_safe, axis=0) * valid
        outs_real.append(jnp.sum(h_real * piece_real - h_imag * piece_imag, axis=0))
        outs_imag.append(jnp.sum(h_real * piece_imag + h_imag * piece_real, axis=0))
    spec_real = jnp.stack(outs_real)
    spec_imag = jnp.stack(outs_imag)
    back_angle = angle_table(seg, width, width)
    conv = jnp.einsum("tk,bkc->btc", jnp.cos(back_angle), spec_real, precision=highest)
    conv = conv - jnp.einsum("tk,bkc->btc", jnp.sin(back_angle), spec_imag, precision=highest)
    conv = (conv / width).reshape(2 * seg, chans)
    gated = (query * conv).astype(jnp.bfloat16)
    share = lax.psum_scatter(
        lax.dot_general(
            out_weight, gated, (((0,), (1,)), ((), ())), preferred_element_type=jnp.float32
        ),
        "chan",
        scatter_dimension=0,
        tiled=True,
    )
    result = share.T.astype(jnp.bfloat16)
    return result


def solution(mesh):
    return jax.shard_map(
        on_device,
        mesh=mesh,
        in_specs=(P("seq", "chan"), P("seq", "chan"), P(None, None, "chan"), P("chan", None), P()),
        out_specs=P("seq", "chan"),
        check_vma=False,
    )
```

profile of v0, /device:TPU:0, one launch (start us, length us, event | category | flops | bytes accessed | tf_op | source)
XLA Modules:
  0.0 136.8 jit_solution(15987896353886890570)
XLA Ops:
  6.5 0.0 copy-start
  6.5 0.0 copy-start.1
  6.5 0.0 all-gather.3.cloned.1.call-start
  6.5 16.9 %all_gather.12 = bf16[64,4096]{1,0:T(8,128)(2,1)S(1)} all-gather(bf16[64,512]{1,0:T(8,128)(2,1)} %param.7), channel_id=1, replica_groups=mesh['seq'=4,'chan'=8] {'chan'}, dimensions={1}, use_global_device_ids=true | all-gather | bytes 589824 | tf_op jit(solution)/shard_map/all_gather | solution.py:28
  23.4 6.8 %convolution_bitcast_fusion.2 = f32[3,64,512]{2,1,0:T(8,128)S(1)} fusion(bf16[3,4096,512]{2,1,0:T(8,128)(2,1)} %param.9, bf16[64,4096]{1,0:T(8,128)(2,1)S(1)} %all_gather.12), kind=kOutput, calls=%fused_computation.8 | convolution fusion | flops 805306368 | bytes 13500416 | tf_op jit(solution)/shard_map/tn,snc->stc/dot_general | solution.py:26
  30.3 1.2 convolution_bitcast_fusion.3
  31.5 0.0 all-gather.3.cloned.1.call-update
  31.5 0.0 all-gather.5.cloned.1.call-start
  31.6 1.2 fusion.1
  32.8 0.0 all-gather.5.cloned.1.call-update
  32.8 0.0 reduce-scatter.2.cloned.1.call-start
  32.9 0.0 copy-done
  32.9 9.0 %all_gather.13 = bf16[256,512]{1,0:T(8,128)(2,1)S(1)} all-gather(bf16[64,512]{1,0:T(8,128)(2,1)S(1)} %copy-done), channel_id=1, replica_groups=mesh['seq'=4,'chan'=8] {'seq'}, dimensions={0}, use_global_device_ids=true | all-gather | bytes 327680 | tf_op jit(solution)/shard_map/all_gather | solution.py:37
  41.9 0.1 convert_element_type.33
  42.0 0.0 copy-done.1
  42.0 0.1 dynamic_slice.3
  42.1 0.1 pad.6.clone
  42.2 0.6 fusion.79
  42.8 1.8 %compare_convert_fusion = (f32[8]{0:T(128)S(1)}, f32[8]{0:T(128)}, pred[8]{0:T(512)(128)(4,1)}, s32[8]{0:T(128)S(1)}, pred[8]{0:T(512)(128)(4,1)}, /*index=5*/s32[8]{0:T(128)S(1)}) fusion(s32[8]{0:T(128)S(1)} %copy-done.1, s32[]{:T(128)} %bitcast.16, s32[]{:T(128)} %bitcast.3), kind=kLoop, calls=%fused_computation.84 | loop fusion | flops 160 | bytes 184 | tf_op jit(solution)/shard_map/convert_element_type | solution.py:55
  44.6 0.1 pad_slice_fusion
  44.6 1.3 convolution_bitcast_fusion.1
  46.0 1.6 %gather_fusion = f32[8,64,512]{2,1,0:T(8,128)} fusion(f32[8,64,512]{2,1,0:T(8,128)S(1)} %convolution_bitcast_fusion.1, s32[1024]{0:T(1024)S(1)} %get-tuple-element.25), kind=kCustom, calls=%fused_computation.clone | custom fusion | bytes 2097184 | tf_op jit(solution)/shard_map/jit(_take)/gather | solution.py:57
  47.6 1.3 fusion
  48.9 1.6 %gather_fusion.1 = f32[8,64,512]{2,1,0:T(8,128)} fusion(f32[8,64,512]{2,1,0:T(8,128)S(1)} %fusion, s32[1024]{0:T(1024)S(1)} %get-tuple-element.25), kind=kCustom, calls=%fused_computation.1.clone | custom fusion | bytes 2097184 | tf_op jit(solution)/shard_map/jit(_take)/gather | solution.py:58
  50.5 1.6 %gather_fusion.2 = f32[8,64,512]{2,1,0:T(8,128)} fusion(f32[8,64,512]{2,1,0:T(8,128)S(1)} %convolution_bitcast_fusion.1, s32[1024]{0:T(1024)S(1)} %get-tuple-element.24), kind=kCustom, calls=%fused_computation.2.clone | custom fusion | bytes 2097184 | tf_op jit(solution)/shard_map/jit(_take)/gather | solution.py:57
  52.1 0.6 gather_fusion.3
  52.7 6.7 %all-gather.3.cloned.1.call-done = f32[8,64,512]{2,1,0:T(8,128)} async-done(((f32[2,64,512]{2,1,0:T(8,128)}), f32[8,64,512]{2,1,0:T(8,128)}) %all-gather.3.cloned.1.call-update) | async-done | bytes 1048592 | tf_op jit(solution)/shard_map/all_gather | solution.py:49
  59.4 28.5 %all-gather.5.cloned.1.call-done = f32[8,64,512]{2,1,0:T(8,128)} async-done(((f32[2,64,512]{2,1,0:T(8,128)}), f32[8,64,512]{2,1,0:T(8,128)}) %all-gather.5.cloned.1.call-update) | async-done | bytes 1048592 | tf_op jit(solution)/shard_map/all_gather | solution.py:50
  87.8 3.5 %add_reduce_fusion.1 = (f32[64,512]{1,0:T(8,128)S(1)}, f32[64,512]{1,0:T(8,128)S(1)}, f32[64,512]{1,0:T(8,128)S(1)}, f32[64,512]{1,0:T(8,128)S(1)}) fusion(f32[8,64,512]{2,1,0:T(8,128)} %all-gather.3.cloned.1.call-done, f32[8,64,512]{2,1,0:T(8,128)} %all-gather.5.cloned.1.call-done, f32[8,64,512]{2,1,0:T(8,128)} %gather_fusion, ...), kind=kLoop, calls=%fused_computation.20 | loop fusion | flops 6160384 | bytes 6815824 | tf_op jit(solution)/shard_map/reduce_sum | solution.py:60
  91.3 0.4 fusion.6
  91.7 0.4 fusion.2
  92.1 4.1 %convolution_bitcast_fusion = f32[4096,64]{0,1:T(8,128)} fusion(bf16[64,512]{1,0:T(8,128)(2,1)S(1)} %fusion.14, bf16[512,4096]{1,0:T(8,128)(2,1)} %param.10), kind=kOutput, calls=%fused_computation.4 | convolution fusion | flops 268435456 | bytes 5308416 | tf_op jit(solution)/shard_map/dot_general | solution.py:69
  96.2 0.0 reduce-scatter.2.cloned.1.call-update
  96.2 32.6 %reduce-scatter.2.cloned.1.call-done = f32[512,64]{0,1:T(8,128)} async-done(((f32[4096,64]{0,1:T(8,128)}), f32[512,64]{0,1:T(8,128)}) %reduce-scatter.2.cloned.1.call-update) | async-done | bytes 131088 | tf_op jit(solution)/shard_map/reduce_scatter | solution.py:68
  128.8 1.5 %convert_bitcast_fusion = bf16[64,512]{1,0:T(8,128)(2,1)} fusion(f32[512,64]{0,1:T(8,128)} %reduce-scatter.2.cloned.1.call-done), kind=kLoop, calls=%fused_computation.38 | loop fusion | flops 32768 | bytes 196608 | tf_op jit(solution)/shard_map/convert_element_type | solution.py:76
  (4 shorter events, 0.1 us)
Async XLA Ops:
  6.5 26.3 %copy-start = (bf16[64,512]{1,0:T(8,128)(2,1)S(1)}, bf16[64,512]{1,0:T(8,128)(2,1)}, u32[]{:S(2)}) copy-start(bf16[64,512]{1,0:T(8,128)(2,1)} %param.8) | copy-start | bytes 196612
  6.5 35.5 %copy-start.1 = (s32[8]{0:T(128)S(1)}, s32[8]{0:T(128)}, u32[]{:S(2)}) copy-start(s32[8]{0:T(128)} %param.11) | copy-start | bytes 100
  6.5 52.8 %all-gather.3.cloned.1.call-start = ((), (), s32[]{:S(2)}) async-start(), calls=%async_computation.1 | async-start | bytes 1310720 | tf_op jit(solution)/shard_map/all_gather | solution.py:49
  31.5 56.3 %all-gather.5.cloned.1.call-start = ((), (), s32[]{:S(2)}) async-start(), calls=%async_computation.2 | async-start | bytes 1310720 | tf_op jit(solution)/shard_map/all_gather | solution.py:50
  32.8 95.9 %reduce-scatter.2.cloned.1.call-start = ((), (), s32[]{:S(2)}) async-start(), calls=%async_computation.3 | async-start | bytes 1179648 | tf_op jit(solution)/shard_map/reduce_scatter | solution.py:68
Sparse Core Ops, SparseCore 0:
  31.6 27.6 all-gather.2
  61.2 26.6 all-gather.4
  96.3 32.3 reduce-scatter.1
where the time goes:
time: 137 us
  waiting for transfers between devices  67.8 us (49%)
  blocking collectives  25.9 us (19%)
  matrix products  16.7 us (12%)
  between operations  13.2 us (10%)
  other arithmetic  6.94 us (5%)
  local copies, waits for them, and re-layouts  6.24 us (5%)
    reduce_scatter x1, waiting for transfers between devices, on_device(): lax.psum_scatter(lax.dot_general(out_weight, gated, (((0,), (1,)), ((), (...  32.6 us
    all_gather x1, waiting for transfers between devices, on_device(): piece_imag = lax.all_gather(own_imag, 'seq', axis=0, tiled=True)  28.5 us
    all_gather x1, blocking collectives, on_device(): lax.all_gather(hidden, 'chan', axis=1, tiled=True)  16.9 us
    all_gather x1, blocking collectives, on_device(): lax.all_gather(filters, 'seq', axis=0, tiled=True).astype(jnp.float32)  9 us
    dot_general x1, matrix products, on_device(): jnp.einsum('tn,snc->stc', lax.all_gather(hidden, 'chan', axis=1, tiled=Tr...  6.81 us
    all_gather x1, waiting for transfers between devices, on_device(): piece_real = lax.all_gather(own_real, 'seq', axis=0, tiled=True)  6.66 us
    dot_general x1, matrix products, on_device(): lax.dot_general(out_weight, gated, (((0,), (1,)), ((), ())), preferred_el...  4.05 us
    reduce_sum x1, other arithmetic, on_device(): outs_imag.append(jnp.sum(h_real * piece_imag + h_imag * piece_real, axis=0))  3.47 us
  transfers between devices with their start and end apart: 3, of which 3 were waited for; matrix products, arithmetic and copies ran while one was open for 9% of the time, Pallas kernels for 0%

commit v1 on v0

v1 whole, which is shorter than its diff:
```python
import functools

import jax
import jax.numpy as jnp
from jax import lax
from jax.experimental import pallas as pl
from jax.experimental.pallas import tpu as pltpu
from jax.sharding import PartitionSpec as P

MESH = pl.DeviceIdType.MESH
LANES = 128


def flip(value, bits):
    result, bit = value, 1
    while bit <= bits:
        if bits & bit:
            result = result + bit - 2 * bit * ((value // bit) % 2)
        bit *= 2
    return result


def kernel(
    n_seq,
    n_chan,
    hidden_ref,
    filters_ref,
    win_ref,
    wout_ref,
    table_ref,
    out_ref,
    hbuf,
    fbuf,
    win,
    wout,
    streams,
    fpad,
    msend,
    mrecv,
    mwork,
    acc,
    gated,
    psend,
    precv,
    ssend,
    srecv,
    own_sem,
    win_sem,
    wout_sem,
    hz_send,
    hz_recv,
    hp_send,
    hp_recv,
    f_send,
    f_recv,
    m_send,
    m_recv,
    p_send,
    p_recv,
    s_send,
    s_recv,
):
    rows, chans = hidden_ref.shape
    seg = rows // 2
    tiles = seg // 8
    groups = chans // LANES
    n_z = n_chan // 2
    seq = lax.axis_index("seq")
    chan = lax.axis_index("chan")
    z = chan // 2
    core = chan % 2
    partner = 2 * z + 1 - core

    def chan_of(dz):
        return 2 * flip(z, dz) + core

    def lanes_of(which):
        return pl.ds(pl.multiple_of(which * chans, chans), chans)

    def remote(src, dst, send_sem, recv_sem, **where):
        return pltpu.make_async_remote_copy(
            src_ref=src,
            dst_ref=dst,
            send_sem=send_sem,
            recv_sem=recv_sem,
            device_id=where,
            device_id_type=MESH,
        )

    own_hidden = pltpu.make_async_copy(hidden_ref, hbuf.at[z, :, lanes_of(core)], own_sem.at[0])
    own_filters = pltpu.make_async_copy(filters_ref, fbuf.at[seq], own_sem.at[1])
    own_hidden.start()
    own_filters.start()
    win_copies = []
    for dz in range(n_z):
        part = pl.ds(pl.multiple_of(flip(z, dz) * 2 * chans, 2 * chans), 2 * chans)
        copy = pltpu.make_async_copy(win_ref.at[:, part, :], win.at[:, part, :], win_sem.at[dz])
        copy.start()
        win_copies.append(copy)
    wout_copy = pltpu.make_async_copy(wout_ref, wout, wout_sem)
    wout_copy.start()

    barrier = pltpu.get_barrier_semaphore()
    for ds in range(1, n_seq):
        pl.semaphore_signal(barrier, inc=1, device_id={"seq": flip(seq, ds)}, device_id_type=MESH)
    for dz in range(1, n_z):
        pl.semaphore_signal(barrier, inc=1, device_id={"chan": chan_of(dz)}, device_id_type=MESH)
    pl.semaphore_signal(barrier, inc=1, device_id={"chan": partner}, device_id_type=MESH)
    pl.semaphore_wait(barrier, n_seq - 1 + n_z)

    pending = []
    to_chip = {}
    for dz in range(n_z - 1, 0, -1):
        copy = remote(
            hidden_ref, hbuf.at[z, :, lanes_of(core)], hz_send.at[dz - 1], hz_recv.at[dz - 1], chan=chan_of(dz)
        )
        copy.start()
        to_chip[dz] = copy
        pending.append(copy)
    to_partner = {}
    to_partner[0] = remote(
        hidden_ref, hbuf.at[z, :, lanes_of(core)], hp_send.at[0], hp_recv.at[0], chan=partner
    )
    to_partner[0].start()
    pending.append(to_partner[0])
    filter_copies = []
    for ds in range(1, n_seq):
        copy = remote(filters_ref, fbuf.at[seq], f_send.at[ds - 1], f_recv.at[ds - 1], seq=flip(seq, ds))
        copy.start()
        filter_copies.append(copy)
        pending.append(copy)

    def project(dz, which):
        chip = flip(z, dz)
        part = pl.ds(pl.multiple_of(chip * 2 * chans, 2 * chans), 2 * chans)
        total = jnp.dot(hbuf[chip], win[which, part, :], preferred_element_type=jnp.float32)
        if dz == 0:
            streams[which] = total
        else:
            streams[which] += total

    def unpack_filters():
        own_filters.wait()
        for copy in filter_copies:
            copy.wait_recv()
        for group in range(groups):
            lanes = slice(group * LANES, (group + 1) * LANES)
            fpad[group, 0:seg, :] = jnp.zeros((seg, LANES), jnp.float32)
            for piece in range(n_seq):
                fpad[group, seg + piece * rows : seg + (piece + 1) * rows, :] = fbuf[piece, :, lanes].astype(
                    jnp.float32
                )

    own_hidden.wait()
    for dz in range(n_z):
        if dz:
            chip = flip(z, dz)
            to_chip[dz].wait_recv()
            spot = hbuf.at[chip, :, lanes_of(core)]
            to_partner[dz] = remote(spot, spot, hp_send.at[dz], hp_recv.at[dz], chan=partner)
            to_partner[dz].start()
            pending.append(to_partner[dz])
        if dz == n_z - 1:
            unpack_filters()
        to_partner[dz].wait_recv()
        win_copies[dz].wait()
        project(dz, 1)
        project(dz, 2)
        if dz < n_z - 1:
            project(dz, 0)

    first = table_ref[2 * seq]
    second = table_ref[2 * seq + 1]
    early = jnp.minimum(first, second)
    in_order = jnp.full((seg, LANES), first) < jnp.full((seg, LANES), second)
    for group in range(groups):
        lanes = slice(group * LANES, (group + 1) * LANES)
        product = streams[1, :, lanes] * streams[2, :, lanes]
        lead = jnp.where(in_order, product[:seg], product[seg:])
        tail = jnp.where(in_order, product[seg:], product[:seg])
        mwork[0, group] = lead
        mwork[1, group] = tail
        msend[0:seg, lanes] = lead.astype(jnp.bfloat16)
        msend[seg : 2 * seg, lanes] = tail.astype(jnp.bfloat16)
    m_copies = []
    for ds in range(1, n_seq):
        copy = remote(msend, mrecv.at[ds - 1], m_send.at[ds - 1], m_recv.at[ds - 1], seq=flip(seq, ds))
        copy.start()
        m_copies.append(copy)
        pending.append(copy)
    project(n_z - 1, 0)

    def convolve(totals, group, slot, lag, lower=False):
        base = lag * seg + seg
        totals = list(totals)
        for shift in range(8):
            window = {}
            for gap in range(0 if lower else 1 - tiles, tiles):
                window[gap] = fpad[group, pl.ds(base + (8 * gap - shift), 8), :]
            for b in range(tiles):
                row = 8 * b + shift
                value = jnp.broadcast_to(mwork[slot, group, row : row + 1, :], (8, LANES))
                for a in range(b if lower else 0, tiles):
                    totals[a] = totals[a] + window[a - b] * value
        return totals

    def zeros():
        return [jnp.zeros((8, LANES), jnp.float32) for _ in range(tiles)]

    count = 2 * n_seq

    def own_blocks(group, carry):
        lead = convolve(zeros(), group, 0, 0, lower=True)
        tail = convolve(zeros(), group, 1, 0, lower=True)
        tail = convolve(tail, group, 0, count - 1 - 2 * early)
        for a in range(tiles):
            acc[0, group, 8 * a : 8 * a + 8, :] = lead[a]
            acc[1, group, 8 * a : 8 * a + 8, :] = tail[a]
        return carry

    lax.fori_loop(0, groups, own_blocks, 0)

    for ds in range(1, n_seq):
        other = flip(seq, ds)
        theirs = jnp.minimum(table_ref[2 * other], table_ref[2 * other + 1])
        m_copies[ds - 1].wait_recv()
        later = jnp.full((seg, LANES), early) > jnp.full((seg, LANES), theirs)
        later_tile = jnp.full((8, LANES), early) > jnp.full((8, LANES), theirs)
        for group in range(groups):
            lanes = slice(group * LANES, (group + 1) * LANES)
            lead = mrecv[ds - 1, 0:seg, lanes].astype(jnp.float32)
            tail = mrecv[ds - 1, seg : 2 * seg, lanes].astype(jnp.float32)
            mwork[0, group] = lead
            mwork[1, group] = jnp.where(later, lead, tail)

        def other_blocks(group, carry):
            tail = [acc[1, group, 8 * a : 8 * a + 8, :] for a in range(tiles)]
            tail = convolve(tail, group, 0, count - 1 - early - theirs)
            mixed = convolve(zeros(), group, 1, jnp.maximum(early, theirs) - jnp.minimum(early, theirs))
            for a in range(tiles):
                place = slice(8 * a, 8 * a + 8)
                acc[0, group, place, :] += jnp.where(later_tile, mixed[a], 0.0)
                acc[1, group, place, :] = tail[a] + jnp.where(later_tile, 0.0, mixed[a])
            return carry

        lax.fori_loop(0, groups, other_blocks, 0)

    for group in range(groups):
        lanes = slice(group * LANES, (group + 1) * LANES)
        lead = acc[0, group]
        tail = acc[1, group]
        gated[0:seg, lanes] = (streams[0, 0:seg, lanes] * jnp.where(in_order, lead, tail)).astype(jnp.bfloat16)
        gated[seg : 2 * seg, lanes] = (
            streams[0, seg : 2 * seg, lanes] * jnp.where(in_order, tail, lead)
        ).astype(jnp.bfloat16)

    wout_copy.wait()
    order = list(range(n_z - 1, -1, -1))
    p_copies = {}
    for dz in order:
        columns = lanes_of(2 * flip(z, dz) + 1 - core)
        psend[dz] = jnp.dot(gated[...], wout[:, columns], preferred_element_type=jnp.float32).astype(
            jnp.bfloat16
        )
        p_copies[dz] = remote(psend.at[dz], precv.at[dz], p_send.at[dz], p_recv.at[dz], chan=partner)
        p_copies[dz].start()
        pending.append(p_copies[dz])
    s_copies = []
    for dz in order:
        columns = lanes_of(chan_of(dz))
        share = jnp.dot(gated[...], wout[:, columns], preferred_element_type=jnp.float32)
        p_copies[dz].wait_recv()
        share = share + precv[dz].astype(jnp.float32)
        if dz:
            ssend[dz - 1] = share.astype(jnp.bfloat16)
            copy = remote(
                ssend.at[dz - 1], srecv.at[dz - 1], s_send.at[dz - 1], s_recv.at[dz - 1], chan=chan_of(dz)
            )
            copy.start()
            s_copies.append(copy)
            pending.append(copy)
        else:
            streams[0] = share
    for copy in s_copies:
        copy.wait_recv()
    total = streams[0]
    for dz in range(1, n_z):
        total = total + srecv[dz - 1].astype(jnp.float32)
    out_ref[...] = total.astype(jnp.bfloat16)
    for copy in pending:
        copy.wait_send()


def on_device(n_seq, n_chan, hidden, filters, in_weight, out_weight, block_table):
    rows, chans = hidden.shape
    seg = rows // 2
    groups = chans // LANES
    n_z = n_chan // 2
    width = in_weight.shape[1]
    bf16, f32 = jnp.bfloat16, jnp.float32
    dma = pltpu.SemaphoreType.DMA
    anywhere = pl.BlockSpec(memory_space=pl.ANY)
    return pl.pallas_call(
        functools.partial(kernel, n_seq, n_chan),
        out_shape=jax.ShapeDtypeStruct((rows, chans), bf16),
        in_specs=[anywhere] * 4 + [pl.BlockSpec(memory_space=pltpu.SMEM)],
        out_specs=pl.BlockSpec(memory_space=pltpu.VMEM),
        scratch_shapes=[
            pltpu.VMEM((n_z, rows, 2 * chans), bf16),
            pltpu.VMEM((n_seq, rows, chans), bf16),
            pltpu.VMEM((3, width, chans), bf16),
            pltpu.VMEM((chans, width), bf16),
            pltpu.VMEM((3, rows, chans), f32),
            pltpu.VMEM((groups, seg + n_seq * rows, LANES), f32),
            pltpu.VMEM((rows, chans), bf16),
            pltpu.VMEM((n_seq - 1, rows, chans), bf16),
            pltpu.VMEM((2, groups, seg, LANES), f32),
            pltpu.VMEM((2, groups, seg, LANES), f32),
            pltpu.VMEM((rows, chans), bf16),
            pltpu.VMEM((n_z, rows, chans), bf16),
            pltpu.VMEM((n_z, rows, chans), bf16),
            pltpu.VMEM((n_z - 1, rows, chans), bf16),
            pltpu.VMEM((n_z - 1, rows, chans), bf16),
            dma((2,)),
            dma((n_z,)),
            dma,
            dma((n_z - 1,)),
            dma((n_z - 1,)),
            dma((n_z,)),
            dma((n_z,)),
            dma((n_seq - 1,)),
            dma((n_seq - 1,)),
            dma((n_seq - 1,)),
            dma((n_seq - 1,)),
            dma((n_z,)),
            dma((n_z,)),
            dma((n_z - 1,)),
            dma((n_z - 1,)),
        ],
        compiler_params=pltpu.CompilerParams(
            collective_id=0, has_side_effects=True, vmem_limit_bytes=40 * 1024 * 1024
        ),
        cost_estimate=pl.CostEstimate(
            flops=8 * rows * width * chans, bytes_accessed=8 * width * chans, transcendentals=0
        ),
    )(hidden, filters, in_weight, out_weight, block_table)


def solution(mesh):
    return jax.shard_map(
        functools.partial(on_device, mesh.shape["seq"], mesh.shape["chan"]),
        mesh=mesh,
        in_specs=(P("seq", "chan"), P("seq", "chan"), P(None, None, "chan"), P("chan", None), P()),
        out_specs=P("seq", "chan"),
        check_vma=False,
    )
```

time: 137 us -> 37 us (0.27)
  waiting for transfers between devices: 67.8 us -> 0 us
  Pallas kernels: 0 us -> 31.6 us
  blocking collectives: 25.9 us -> 0 us
  matrix products: 16.7 us -> 0 us
  between operations: 13.2 us -> 0.01 us
  other arithmetic: 6.94 us -> 0 us
    all_gather x2 -> x0, waiting for transfers between devices: 35.2 us -> none  [the longest x1 28.5 us: on_device(): piece_imag = lax.all_gather(own_imag, 'seq', axis=0, tiled=True)]
    reduce_scatter x1 -> x0, waiting for transfers between devices: 32.6 us -> none  [on_device(): lax.psum_scatter(lax.dot_general(out_weight, gated, (((0,), (1,)), ((), (...]
    pallas_call x0 -> x1, Pallas kernels: none -> 31.6 us  [on_device(): pl.pallas_call(functools.partial(kernel, n_seq, n_chan), out_shape=jax.Sh...]
    all_gather x2 -> x0, blocking collectives: 25.9 us -> none  [the longest x1 16.9 us: on_device(): lax.all_gather(hidden, 'chan', axis=1, tiled=True)]
    dot_general x8 -> x0, matrix products: 16.7 us -> none  [the longest x1 6.81 us: on_device(): jnp.einsum('tn,snc->stc', lax.all_gather(hidden, 'chan', axis=1, tiled=Tr...]
    gather x4 -> x0, local copies, waits for them, and re-layouts: 5.41 us -> none  [the longest x2 3.19 us: on_device(): h_real = jnp.take(filt_real, lag_safe, axis=0) * valid]
    unnamed x4 -> x9, local copies, waits for them, and re-layouts: 0.01 us -> 5.15 us
    reduce_sum x1 -> x0, other arithmetic: 3.47 us -> none  [on_device(): outs_imag.append(jnp.sum(h_real * piece_imag + h_imag * piece_real, axis=0))]
  transfers between devices with their start and end apart: 3 -> 0, of which waited for: 3 -> 0; matrix products, arithmetic and copies ran while one was open for 9% -> 0% of each run, Pallas kernels for 0% -> 0%
where the time goes in v1:
time: 37 us; the launch traced here: 36.8 us
  Pallas kernels  31.6 us (85%)
  local copies, waits for them, and re-layouts  5.15 us (14%)
    pallas_call x1, Pallas kernels, on_device(): pl.pallas_call(functools.partial(kernel, n_seq, n_chan), out_shape=jax.Sh...  31.6 us
    unnamed x9, local copies, waits for them, and re-layouts  5.15 us

profile of v1, /device:TPU:0, one launch (start us, length us, event | category | flops | bytes accessed | tf_op | source)
XLA Modules:
  0.0 36.8 jit_solution(15237939554770443869)
XLA Ops:
  0.0 0.0 copy-start
  0.0 2.2 %copy-done = bf16[512,4096]{1,0:T(8,128)(2,1)S(1)} copy-done((bf16[512,4096]{1,0:T(8,128)(2,1)S(1)}, bf16[512,4096]{1,0:T(8,128)(2,1)}, u32[]{:S(2)}) %copy-start) | copy-done | bytes 4194328
  2.2 0.0 copy-start.1
  2.2 0.8 %copy-done.1 = bf16[64,512]{1,0:T(8,128)(2,1)S(1)} copy-done((bf16[64,512]{1,0:T(8,128)(2,1)S(1)}, bf16[64,512]{1,0:T(8,128)(2,1)}, u32[]{:S(2)}) %copy-start.1) | copy-done | bytes 65560
  3.0 0.0 copy-start.2
  3.0 0.8 %copy-done.2 = bf16[64,512]{1,0:T(8,128)(2,1)S(1)} copy-done((bf16[64,512]{1,0:T(8,128)(2,1)S(1)}, bf16[64,512]{1,0:T(8,128)(2,1)}, u32[]{:S(2)}) %copy-start.2) | copy-done | bytes 65560
  3.9 0.0 copy-start.3
  3.9 0.7 %copy-done.3 = s32[8]{0:T(128)S(1)} copy-done((s32[8]{0:T(128)S(1)}, s32[8]{0:T(128)}, u32[]{:S(2)}) %copy-start.3) | copy-done | bytes 56
  4.5 31.6 %shard_map.55 = bf16[64,512]{1,0:T(8,128)(2,1)S(1)} custom-call(bf16[64,512]{1,0:T(8,128)(2,1)S(1)} %copy-done.1, bf16[64,512]{1,0:T(8,128)(2,1)S(1)} %copy-done.2, bf16[3,4096,512]{2,1,0:T(8,128)(2,1)} %win_ref.1, bf16[512,4096]{1,0:T(8,128)(2,1)S(1)} %copy-done, s32[8]{0:T(128)S(1)} %copy-done.3), custom_call_target="tpu_custom_call" | custom-call | flops 1073741824 | bytes 16777216 | tf_op jit(solution)/shard_map/pallas_call | solution.py:303
  36.1 0.6 %copy.7 = bf16[64,512]{1,0:T(8,128)(2,1)} copy(bf16[64,512]{1,0:T(8,128)(2,1)S(1)} %shard_map.55) | data formatting | bytes 131072
Async XLA Ops:
  0.0 2.2 %copy-start = (bf16[512,4096]{1,0:T(8,128)(2,1)S(1)}, bf16[512,4096]{1,0:T(8,128)(2,1)}, u32[]{:S(2)}) copy-start(bf16[512,4096]{1,0:T(8,128)(2,1)} %wout_ref.1) | copy-start | bytes 12582916
  2.2 0.8 %copy-start.1 = (bf16[64,512]{1,0:T(8,128)(2,1)S(1)}, bf16[64,512]{1,0:T(8,128)(2,1)}, u32[]{:S(2)}) copy-start(bf16[64,512]{1,0:T(8,128)(2,1)} %hidden_ref.1) | copy-start | bytes 196612
  3.0 0.8 %copy-start.2 = (bf16[64,512]{1,0:T(8,128)(2,1)S(1)}, bf16[64,512]{1,0:T(8,128)(2,1)}, u32[]{:S(2)}) copy-start(bf16[64,512]{1,0:T(8,128)(2,1)} %filters_ref.1) | copy-start | bytes 196612
  3.9 0.7 %copy-start.3 = (s32[8]{0:T(128)S(1)}, s32[8]{0:T(128)}, u32[]{:S(2)}) copy-start(s32[8]{0:T(128)} %table_ref.1) | copy-start | bytes 100

commit v2 on v1

--- a/solution.py
+++ b/solution.py
@@ -27,8 +27,9 @@
     filters_ref,
     win_ref,
     wout_ref,
+    table_hbm,
+    out_ref,
     table_ref,
-    out_ref,
     hbuf,
     fbuf,
     win,
@@ -89,6 +90,8 @@
 
     own_hidden = pltpu.make_async_copy(hidden_ref, hbuf.at[z, :, lanes_of(core)], own_sem.at[0])
     own_filters = pltpu.make_async_copy(filters_ref, fbuf.at[seq], own_sem.at[1])
+    own_table = pltpu.make_async_copy(table_hbm, table_ref, own_sem.at[2])
+    own_table.start()
     own_hidden.start()
     own_filters.start()
     win_copies = []
@@ -169,6 +172,7 @@
         if dz < n_z - 1:
             project(dz, 0)
 
+    own_table.wait()
     first = table_ref[2 * seq]
     second = table_ref[2 * seq + 1]
     early = jnp.minimum(first, second)
@@ -299,13 +303,14 @@
     width = in_weight.shape[1]
     bf16, f32 = jnp.bfloat16, jnp.float32
     dma = pltpu.SemaphoreType.DMA
-    anywhere = pl.BlockSpec(memory_space=pl.ANY)
+    in_hbm = pl.BlockSpec(memory_space=pltpu.HBM)
     return pl.pallas_call(
         functools.partial(kernel, n_seq, n_chan),
         out_shape=jax.ShapeDtypeStruct((rows, chans), bf16),
-        in_specs=[anywhere] * 4 + [pl.BlockSpec(memory_space=pltpu.SMEM)],
+        in_specs=[in_hbm] * 5,
         out_specs=pl.BlockSpec(memory_space=pltpu.VMEM),
         scratch_shapes=[
+            pltpu.SMEM(block_table.shape, jnp.int32),
             pltpu.VMEM((n_z, rows, 2 * chans), bf16),
             pltpu.VMEM((n_seq, rows, chans), bf16),
             pltpu.VMEM((3, width, chans), bf16),
@@ -321,7 +326,7 @@
             pltpu.VMEM((n_z, rows, chans), bf16),
             pltpu.VMEM((n_z - 1, rows, chans), bf16),
             pltpu.VMEM((n_z - 1, rows, chans), bf16),
-            dma((2,)),
+            dma((3,)),
             dma((n_z,)),
             dma,
             dma((n_z - 1,)),
@@ -338,7 +343,7 @@
             dma((n_z - 1,)),
         ],
         compiler_params=pltpu.CompilerParams(
-            collective_id=0, has_side_effects=True, vmem_limit_bytes=40 * 1024 * 1024
+            collective_id=0, has_side_effects=True, vmem_limit_bytes=64 * 1024 * 1024
         ),
         cost_estimate=pl.CostEstimate(
             flops=8 * rows * width * chans, bytes_accessed=8 * width * chans, transcendentals=0

time: 37 us -> 33.1 us (0.89)
  local copies, waits for them, and re-layouts: 5.15 us -> 1.47 us
    unnamed x9 -> x1, local copies, waits for them, and re-layouts: 5.15 us -> 1.47 us
where the time goes in v2:
time: 33.1 us; the launch traced here: 33 us
  Pallas kernels  31.5 us (95%)
  local copies, waits for them, and re-layouts  1.47 us (4%)
    pallas_call x1, Pallas kernels, on_device(): pl.pallas_call(functools.partial(kernel, n_seq, n_chan), out_shape=jax.Sh...  31.5 us
    unnamed x1, local copies, waits for them, and re-layouts  1.47 us

profile of v2, /device:TPU:0, one launch (start us, length us, event | category | flops | bytes accessed | tf_op | source)
XLA Modules:
  0.0 33.0 jit_solution(12759579714310426608)
XLA Ops:
  0.0 31.5 %shard_map.55 = bf16[64,512]{1,0:T(8,128)(2,1)} custom-call(bf16[64,512]{1,0:T(8,128)(2,1)} %hidden_ref.1, bf16[64,512]{1,0:T(8,128)(2,1)} %filters_ref.1, bf16[3,4096,512]{2,1,0:T(8,128)(2,1)} %win_ref.1, bf16[512,4096]{1,0:T(8,128)(2,1)} %wout_ref.1, s32[8]{0:T(128)} %table_hbm.1), custom_call_target="tpu_custom_call" | custom-call | flops 1073741824 | bytes 16777216 | tf_op jit(solution)/shard_map/pallas_call | solution.py:307
  31.5 1.5 %copy.7 = bf16[64,512]{1,0:T(8,128)(2,1)} copy(bf16[64,512]{1,0:T(8,128)(2,1)} %shard_map.55) | data formatting | bytes 131072

commit v3 on v2

v3 whole, which is shorter than its diff:
```python
import functools

import jax
import jax.numpy as jnp
from jax import lax
from jax.experimental import pallas as pl
from jax.experimental.pallas import tpu as pltpu
from jax.sharding import PartitionSpec as P

MESH = pl.DeviceIdType.MESH
LANES = 128


def flip(value, bits):
    result, bit = value, 1
    while bit <= bits:
        if bits & bit:
            result = result + bit - 2 * bit * ((value // bit) % 2)
        bit *= 2
    return result


def kernel(
    n_seq,
    n_chan,
    hidden_ref,
    filters_ref,
    win_ref,
    wout_ref,
    table_hbm,
    out_ref,
    table_ref,
    held,
    ordered,
    hbuf,
    fbuf,
    win,
    wout,
    streams,
    fpad,
    msend,
    mrecv,
    mwork,
    acc,
    gated,
    psend,
    precv,
    ssend,
    srecv,
    share_own,
    own_sem,
    win_sem,
    wout_sem,
    hz_send,
    hz_recv,
    hp_send,
    hp_recv,
    f_send,
    f_recv,
    m_send,
    m_recv,
    p_send,
    p_recv,
    s_send,
    s_recv,
):
    rows, chans = hidden_ref.shape
    seg = rows // 2
    tiles = seg // 8
    groups = chans // LANES
    n_z = n_chan // 2
    seq = lax.axis_index("seq")
    chan = lax.axis_index("chan")
    z = chan // 2
    core = chan % 2
    partner = 2 * z + 1 - core

    def chan_of(dz):
        return 2 * flip(z, dz) + core

    def lanes_of(which):
        return pl.ds(pl.multiple_of(which * chans, chans), chans)

    pending = []

    def send(src, dst, send_sem, recv_sem, **where):
        copy = pltpu.make_async_remote_copy(
            src_ref=src,
            dst_ref=dst,
            send_sem=send_sem,
            recv_sem=recv_sem,
            device_id=where,
            device_id_type=MESH,
        )
        copy.start()
        pending.append(copy)
        return copy

    own_table = pltpu.make_async_copy(table_hbm, table_ref, own_sem.at[0])
    own_hidden = pltpu.make_async_copy(hidden_ref, held, own_sem.at[1])
    own_filters = pltpu.make_async_copy(filters_ref, fbuf.at[seq], own_sem.at[2])
    own_table.start()
    own_hidden.start()

    barrier = pltpu.get_barrier_semaphore()
    for ds in range(1, n_seq):
        pl.semaphore_signal(barrier, inc=1, device_id={"seq": flip(seq, ds)}, device_id_type=MESH)
    for dz in range(1, n_z):
        pl.semaphore_signal(barrier, inc=1, device_id={"chan": chan_of(dz)}, device_id_type=MESH)
    pl.semaphore_signal(barrier, inc=1, device_id={"chan": partner}, device_id_type=MESH)

    win_copies = []
    for dz in range(n_z):
        part = pl.ds(pl.multiple_of(flip(z, dz) * 2 * chans, 2 * chans), 2 * chans)
        copy = pltpu.make_async_copy(win_ref.at[:, part, :], win.at[:, part, :], win_sem.at[dz])
        copy.start()
        win_copies.append(copy)
    own_filters.start()
    wout_copy = pltpu.make_async_copy(wout_ref, wout, wout_sem)
    wout_copy.start()

    own_table.wait()
    first = table_ref[2 * seq]
    second = table_ref[2 * seq + 1]
    early = jnp.minimum(first, second)

    def in_order(shape):
        return jnp.full(shape, first) < jnp.full(shape, second)

    own_hidden.wait()
    for group in range(groups):
        lanes = slice(group * LANES, (group + 1) * LANES)
        top = held[0:seg, lanes].astype(jnp.float32)
        bottom = held[seg:rows, lanes].astype(jnp.float32)
        keep = in_order((seg, LANES))
        ordered[0, :, lanes] = jnp.where(keep, top, bottom).astype(jnp.bfloat16)
        ordered[1, :, lanes] = jnp.where(keep, bottom, top).astype(jnp.bfloat16)
    for half in range(2):
        hbuf[half, z, :, lanes_of(core)] = ordered[half]
    pl.semaphore_wait(barrier, n_seq - 1 + n_z)

    to_chip, to_partner = {}, {}
    for half in range(2):
        for dz in range(n_z - 1, 0, -1):
            to_chip[half, dz] = send(
                ordered.at[half],
                hbuf.at[half, z, :, lanes_of(core)],
                hz_send.at[half, dz - 1],
                hz_recv.at[half, dz - 1],
                chan=chan_of(dz),
            )
        to_partner[half, 0] = send(
            ordered.at[half],
            hbuf.at[half, z, :, lanes_of(core)],
            hp_send.at[half, 0],
            hp_recv.at[half, 0],
            chan=partner,
        )
    filter_copies = [
        send(filters_ref, fbuf.at[seq], f_send.at[ds - 1], f_recv.at[ds - 1], seq=flip(seq, ds))
        for ds in range(1, n_seq)
    ]

    def project(half, dz, which):
        chip = flip(z, dz)
        part = pl.ds(pl.multiple_of(chip * 2 * chans, 2 * chans), 2 * chans)
        total = jnp.dot(hbuf[half, chip], win[which, part, :], preferred_element_type=jnp.float32)
        if dz == 0:
            streams[half, which] = total
        else:
            streams[half, which] += total

    m_copies = {}

    def keys_values(half):
        for dz in range(n_z):
            if dz:
                to_chip[half, dz].wait_recv()
                spot = hbuf.at[half, flip(z, dz), :, lanes_of(core)]
                to_partner[half, dz] = send(
                    spot, spot, hp_send.at[half, dz], hp_recv.at[half, dz], chan=partner
                )
            to_partner[half, dz].wait_recv()
            if half == 0:
                win_copies[dz].wait()
            project(half, dz, 1)
            project(half, dz, 2)
        for group in range(groups):
            lanes = slice(group * LANES, (group + 1) * LANES)
            product = streams[half, 1, :, lanes] * streams[half, 2, :, lanes]
            mwork[half, group] = product
            msend[half, :, lanes] = product.astype(jnp.bfloat16)
        for ds in range(1, n_seq):
            m_copies[half, ds] = send(
                msend.at[half],
                mrecv.at[half, ds - 1],
                m_send.at[half, ds - 1],
                m_recv.at[half, ds - 1],
                seq=flip(seq, ds),
            )

    def queries(half):
        for dz in range(n_z):
            project(half, dz, 0)

    def unpack_filters():
        own_filters.wait()
        for copy in filter_copies:
            copy.wait_recv()
        for group in range(groups):
            lanes = slice(group * LANES, (group + 1) * LANES)
            fpad[group, 0 : 2 * seg, :] = jnp.zeros((2 * seg, LANES), jnp.float32)
            for piece in range(n_seq):
                place = slice(2 * seg + piece * rows, 2 * seg + (piece + 1) * rows)
                fpad[group, place, :] = fbuf[piece, :, lanes].astype(jnp.float32)

    def convolve(targets, group, slot, lower=False):
        targets = [(jnp.maximum(lag, -1) * seg + 2 * seg, list(totals)) for lag, totals in targets]
        for shift in range(8):
            values = []
            for b in range(tiles):
                row = 8 * b + shift
                values.append(jnp.broadcast_to(mwork[slot, group, row : row + 1, :], (8, LANES)))
            for base, totals in targets:
                for gap in range(0 if lower else 1 - tiles, tiles):
                    window = fpad[group, pl.ds(base + (8 * gap - shift), 8), :]
                    for b in range(tiles):
                        if 0 <= b + gap < tiles:
                            totals[b + gap] = totals[b + gap] + window * values[b]
        return [totals for _, totals in targets]

    def zeros():
        return [jnp.zeros((8, LANES), jnp.float32) for _ in range(tiles)]

    def load_acc(half, group):
        return [acc[half, group, 8 * a : 8 * a + 8, :] for a in range(tiles)]

    def store_acc(half, group, totals):
        for a in range(tiles):
            acc[half, group, 8 * a : 8 * a + 8, :] = totals[a]

    count = 2 * n_seq
    zero = early * 0

    def own_early(group, carry):
        (lead,) = convolve([(zero, zeros())], group, 0, lower=True)
        (tail,) = convolve([(count - 1 - 2 * early, zeros())], group, 0)
        store_acc(0, group, lead)
        store_acc(1, group, tail)
        return carry

    def own_late(group, carry):
        (tail,) = convolve([(zero, load_acc(1, group))], group, 1, lower=True)
        store_acc(1, group, tail)
        return carry

    def receive(half, ds):
        m_copies[half, ds].wait_recv()
        for group in range(groups):
            lanes = slice(group * LANES, (group + 1) * LANES)
            mwork[1 + ds, group] = mrecv[half, ds - 1, :, lanes].astype(jnp.float32)
        other = flip(seq, ds)
        return jnp.minimum(table_ref[2 * other], table_ref[2 * other + 1])

    def other_early(ds):
        theirs = receive(0, ds)

        def body(group, carry):
            lead, tail = convolve(
                [(early - theirs, load_acc(0, group)), (count - 1 - early - theirs, load_acc(1, group))],
                group,
                1 + ds,
            )
            store_acc(0, group, lead)
            store_acc(1, group, tail)
            return carry

        lax.fori_loop(0, groups, body, 0)

    def other_late(ds):
        theirs = receive(1, ds)

        def body(group, carry):
            (tail,) = convolve([(theirs - early, load_acc(1, group))], group, 1 + ds)
            store_acc(1, group, tail)
            return carry

        lax.fori_loop(0, groups, body, 0)

    order = list(range(n_z - 1, -1, -1))
    p_copies, s_copies = {}, {}

    def for_partner(half):
        for group in range(groups):
            lanes = slice(group * LANES, (group + 1) * LANES)
            gated[half, :, lanes] = (streams[half, 0, :, lanes] * acc[half, group]).astype(jnp.bfloat16)
        for dz in order:
            columns = lanes_of(2 * flip(z, dz) + 1 - core)
            share = jnp.dot(gated[half], wout[:, columns], preferred_element_type=jnp.float32)
            psend[half, dz] = share.astype(jnp.bfloat16)
            p_copies[half, dz] = send(
                psend.at[half, dz],
                precv.at[half, dz],
                p_send.at[half, dz],
                p_recv.at[half, dz],
                chan=partner,
            )

    def for_chips(half):
        for dz in order:
            share = jnp.dot(gated[half], wout[:, lanes_of(chan_of(dz))], preferred_element_type=jnp.float32)
            p_copies[half, dz].wait_recv()
            share = share + precv[half, dz].astype(jnp.float32)
            if dz:
                ssend[half, dz - 1] = share.astype(jnp.bfloat16)
                s_copies[half, dz] = send(
                    ssend.at[half, dz - 1],
                    srecv.at[half, dz - 1],
                    s_send.at[half, dz - 1],
                    s_recv.at[half, dz - 1],
                    chan=chan_of(dz),
                )
            else:
                share_own[half] = share

    def add_up(half):
        total = share_own[half]
        for dz in range(1, n_z):
            s_copies[half, dz].wait_recv()
            total = total + srecv[half, dz - 1].astype(jnp.float32)
        return total

    keys_values(0)
    queries(0)
    unpack_filters()
    lax.fori_loop(0, groups, own_early, 0)
    keys_values(1)
    for ds in range(1, n_seq):
        other_early(ds)
    wout_copy.wait()
    for_partner(0)
    queries(1)
    lax.fori_loop(0, groups, own_late, 0)
    for_chips(0)
    for ds in range(1, n_seq):
        other_late(ds)
    for_partner(1)
    for_chips(1)
    lead = add_up(0)
    tail = add_up(1)
    keep = in_order((seg, chans))
    out_ref[0:seg, :] = jnp.where(keep, lead, tail).astype(jnp.bfloat16)
    out_ref[seg:rows, :] = jnp.where(keep, tail, lead).astype(jnp.bfloat16)
    for copy in pending:
        copy.wait_send()


def on_device(n_seq, n_chan, hidden, filters, in_weight, out_weight, block_table):
    rows, chans = hidden.shape
    seg = rows // 2
    groups = chans // LANES
    n_z = n_chan // 2
    width = in_weight.shape[1]
    bf16, f32 = jnp.bfloat16, jnp.float32
    dma = pltpu.SemaphoreType.DMA
    in_hbm = pl.BlockSpec(memory_space=pltpu.HBM)
    return pl.pallas_call(
        functools.partial(kernel, n_seq, n_chan),
        out_shape=jax.ShapeDtypeStruct((rows, chans), bf16),
        in_specs=[in_hbm] * 5,
        out_specs=pl.BlockSpec(memory_space=pltpu.VMEM),
        scratch_shapes=[
            pltpu.SMEM(block_table.shape, jnp.int32),
            pltpu.VMEM((rows, chans), bf16),
            pltpu.VMEM((2, seg, chans), bf16),
            pltpu.VMEM((2, n_z, seg, 2 * chans), bf16),
            pltpu.VMEM((n_seq, rows, chans), bf16),
            pltpu.VMEM((3, width, chans), bf16),
            pltpu.VMEM((chans, width), bf16),
            pltpu.VMEM((2, 3, seg, chans), f32),
            pltpu.VMEM((groups, 2 * seg + n_seq * rows, LANES), f32),
            pltpu.VMEM((2, seg, chans), bf16),
            pltpu.VMEM((2, n_seq - 1, seg, chans), bf16),
            pltpu.VMEM((n_seq + 1, groups, seg, LANES), f32),
            pltpu.VMEM((2, groups, seg, LANES), f32),
            pltpu.VMEM((2, seg, chans), bf16),
            pltpu.VMEM((2, n_z, seg, chans), bf16),
            pltpu.VMEM((2, n_z, seg, chans), bf16),
            pltpu.VMEM((2, n_z - 1, seg, chans), bf16),
            pltpu.VMEM((2, n_z - 1, seg, chans), bf16),
            pltpu.VMEM((2, seg, chans), f32),
            dma((3,)),
            dma((n_z,)),
            dma,
            dma((2, n_z - 1)),
            dma((2, n_z - 1)),
            dma((2, n_z)),
            dma((2, n_z)),
            dma((n_seq - 1,)),
            dma((n_seq - 1,)),
            dma((2, n_seq - 1)),
            dma((2, n_seq - 1)),
            dma((2, n_z)),
            dma((2, n_z)),
            dma((2, n_z - 1)),
            dma((2, n_z - 1)),
        ],
        compiler_params=pltpu.CompilerParams(
            collective_id=0, has_side_effects=True, vmem_limit_bytes=64 * 1024 * 1024
        ),
        cost_estimate=pl.CostEstimate(
            flops=8 * rows * width * chans, bytes_accessed=8 * width * chans, transcendentals=0
        ),
    )(hidden, filters, in_weight, out_weight, block_table)


def solution(mesh):
    return jax.shard_map(
        functools.partial(on_device, mesh.shape["seq"], mesh.shape["chan"]),
        mesh=mesh,
        in_specs=(P("seq", "chan"), P("seq", "chan"), P(None, None, "chan"), P("chan", None), P()),
        out_specs=P("seq", "chan"),
        check_vma=False,
    )
```

time: 33.1 us -> 34.2 us (1.033)
  Pallas kernels: 31.5 us -> 32.5 us
    pallas_call x1, Pallas kernels: 31.5 us -> 32.5 us  [on_device(): pl.pallas_call(functools.partial(kernel, n_seq, n_chan), out_shape=jax.Sh...]
where the time goes in v3:
time: 34.2 us; the launch traced here: 34 us
  Pallas kernels  32.5 us (95%)
  local copies, waits for them, and re-layouts  1.47 us (4%)
    pallas_call x1, Pallas kernels, on_device(): pl.pallas_call(functools.partial(kernel, n_seq, n_chan), out_shape=jax.Sh...  32.5 us
    unnamed x1, local copies, waits for them, and re-layouts  1.47 us

profile of v3, /device:TPU:0, one launch (start us, length us, event | category | flops | bytes accessed | tf_op | source)
XLA Modules:
  0.0 34.0 jit_solution(12311402366612941365)
XLA Ops:
  0.0 32.5 %shard_map.55 = bf16[64,512]{1,0:T(8,128)(2,1)} custom-call(bf16[64,512]{1,0:T(8,128)(2,1)} %hidden_ref.1, bf16[64,512]{1,0:T(8,128)(2,1)} %filters_ref.1, bf16[3,4096,512]{2,1,0:T(8,128)(2,1)} %win_ref.1, bf16[512,4096]{1,0:T(8,128)(2,1)} %wout_ref.1, s32[8]{0:T(128)} %table_hbm.1), custom_call_target="tpu_custom_call" | custom-call | flops 1073741824 | bytes 16777216 | tf_op jit(solution)/shard_map/pallas_call | solution.py:367
  32.5 1.5 %copy.7 = bf16[64,512]{1,0:T(8,128)(2,1)} copy(bf16[64,512]{1,0:T(8,128)(2,1)} %shard_map.55) | data formatting | bytes 131072

commit v4 on v3

--- a/solution.py
+++ b/solution.py
@@ -109,15 +109,19 @@
         pl.semaphore_signal(barrier, inc=1, device_id={"chan": chan_of(dz)}, device_id_type=MESH)
     pl.semaphore_signal(barrier, inc=1, device_id={"chan": partner}, device_id_type=MESH)
 
-    win_copies = []
+    kv_copies, q_copies = [], []
     for dz in range(n_z):
         part = pl.ds(pl.multiple_of(flip(z, dz) * 2 * chans, 2 * chans), 2 * chans)
-        copy = pltpu.make_async_copy(win_ref.at[:, part, :], win.at[:, part, :], win_sem.at[dz])
+        kv_copies.append(
+            pltpu.make_async_copy(win_ref.at[1:3, part, :], win.at[1:3, part, :], win_sem.at[0, dz])
+        )
+        q_copies.append(
+            pltpu.make_async_copy(win_ref.at[0:1, part, :], win.at[0:1, part, :], win_sem.at[1, dz])
+        )
+    for copy in kv_copies:
         copy.start()
-        win_copies.append(copy)
     own_filters.start()
     wout_copy = pltpu.make_async_copy(wout_ref, wout, wout_sem)
-    wout_copy.start()
 
     own_table.wait()
     first = table_ref[2 * seq]
@@ -133,75 +137,68 @@
         top = held[0:seg, lanes].astype(jnp.float32)
         bottom = held[seg:rows, lanes].astype(jnp.float32)
         keep = in_order((seg, LANES))
-        ordered[0, :, lanes] = jnp.where(keep, top, bottom).astype(jnp.bfloat16)
-        ordered[1, :, lanes] = jnp.where(keep, bottom, top).astype(jnp.bfloat16)
-    for half in range(2):
-        hbuf[half, z, :, lanes_of(core)] = ordered[half]
+        ordered[0:seg, lanes] = jnp.where(keep, top, bottom).astype(jnp.bfloat16)
+        ordered[seg:rows, lanes] = jnp.where(keep, bottom, top).astype(jnp.bfloat16)
+    hbuf[z, :, lanes_of(core)] = ordered[...]
     pl.semaphore_wait(barrier, n_seq - 1 + n_z)
 
     to_chip, to_partner = {}, {}
-    for half in range(2):
-        for dz in range(n_z - 1, 0, -1):
-            to_chip[half, dz] = send(
-                ordered.at[half],
-                hbuf.at[half, z, :, lanes_of(core)],
-                hz_send.at[half, dz - 1],
-                hz_recv.at[half, dz - 1],
-                chan=chan_of(dz),
-            )
-        to_partner[half, 0] = send(
-            ordered.at[half],
-            hbuf.at[half, z, :, lanes_of(core)],
-            hp_send.at[half, 0],
-            hp_recv.at[half, 0],
-            chan=partner,
+    for dz in range(n_z - 1, 0, -1):
+        to_chip[dz] = send(
+            ordered, hbuf.at[z, :, lanes_of(core)], hz_send.at[dz - 1], hz_recv.at[dz - 1], chan=chan_of(dz)
         )
+    to_partner[0] = send(ordered, hbuf.at[z, :, lanes_of(core)], hp_send.at[0], hp_recv.at[0], chan=partner)
     filter_copies = [
         send(filters_ref, fbuf.at[seq], f_send.at[ds - 1], f_recv.at[ds - 1], seq=flip(seq, ds))
         for ds in range(1, n_seq)
     ]
 
-    def project(half, dz, which):
+    def project(dz, which):
         chip = flip(z, dz)
         part = pl.ds(pl.multiple_of(chip * 2 * chans, 2 * chans), 2 * chans)
-        total = jnp.dot(hbuf[half, chip], win[which, part, :], preferred_element_type=jnp.float32)
+        total = jnp.dot(hbuf[chip], win[which, part, :], preferred_element_type=jnp.float32)
         if dz == 0:
-            streams[half, which] = total
+            streams[which] = total
         else:
-            streams[half, which] += total
+            streams[which] += total
 
     m_copies = {}
 
-    def keys_values(half):
+    def keys_values():
         for dz in range(n_z):
             if dz:
-                to_chip[half, dz].wait_recv()
-                spot = hbuf.at[half, flip(z, dz), :, lanes_of(core)]
-                to_partner[half, dz] = send(
-                    spot, spot, hp_send.at[half, dz], hp_recv.at[half, dz], chan=partner
+                to_chip[dz].wait_recv()
+                spot = hbuf.at[flip(z, dz), :, lanes_of(core)]
+                to_partner[dz] = send(spot, spot, hp_send.at[dz], hp_recv.at[dz], chan=partner)
+            to_partner[dz].wait_recv()
+            kv_copies[dz].wait()
+            project(dz, 1)
+            project(dz, 2)
+            if dz == 0:
+                for copy in q_copies:
+                    copy.start()
+            if dz == min(1, n_z - 1):
+                wout_copy.start()
+        for half in range(2):
+            part = slice(half * seg, (half + 1) * seg)
+            for group in range(groups):
+                lanes = slice(group * LANES, (group + 1) * LANES)
+                product = streams[1, part, lanes] * streams[2, part, lanes]
+                mwork[half, group] = product
+                msend[half, :, lanes] = product.astype(jnp.bfloat16)
+            for ds in range(1, n_seq):
+                m_copies[half, ds] = send(
+                    msend.at[half],
+                    mrecv.at[half, ds - 1],
+                    m_send.at[half, ds - 1],
+                    m_recv.at[half, ds - 1],
+                    seq=flip(seq, ds),
                 )
-            to_partner[half, dz].wait_recv()
-            if half == 0:
-                win_copies[dz].wait()
-            project(half, dz, 1)
-            project(half, dz, 2)
-        for group in range(groups):
-            lanes = slice(group * LANES, (group + 1) * LANES)
-            product = streams[half, 1, :, lanes] * streams[half, 2, :, lanes]
-            mwork[half, group] = product
-            msend[half, :, lanes] = product.astype(jnp.bfloat16)
-        for ds in range(1, n_seq):
-            m_copies[half, ds] = send(
-                msend.at[half],
-                mrecv.at[half, ds - 1],
-                m_send.at[half, ds - 1],
-                m_recv.at[half, ds - 1],
-                seq=flip(seq, ds),
-            )
-
-    def queries(half):
+
+    def queries():
         for dz in range(n_z):
-            project(half, dz, 0)
+            q_copies[dz].wait()
+            project(dz, 0)
 
     def unpack_filters():
         own_filters.wait()
@@ -290,64 +287,49 @@
     order = list(range(n_z - 1, -1, -1))
     p_copies, s_copies = {}, {}
 
-    def for_partner(half):
-        for group in range(groups):
-            lanes = slice(group * LANES, (group + 1) * LANES)
-            gated[half, :, lanes] = (streams[half, 0, :, lanes] * acc[half, group]).astype(jnp.bfloat16)
+    def for_partner():
+        for half in range(2):
+            part = slice(half * seg, (half + 1) * seg)
+            for group in range(groups):
+                lanes = slice(group * LANES, (group + 1) * LANES)
+                gated[part, lanes] = (streams[0, part, lanes] * acc[half, group]).astype(jnp.bfloat16)
         for dz in order:
             columns = lanes_of(2 * flip(z, dz) + 1 - core)
-            share = jnp.dot(gated[half], wout[:, columns], preferred_element_type=jnp.float32)
-            psend[half, dz] = share.astype(jnp.bfloat16)
-            p_copies[half, dz] = send(
-                psend.at[half, dz],
-                precv.at[half, dz],
-                p_send.at[half, dz],
-                p_recv.at[half, dz],
-                chan=partner,
-            )
-
-    def for_chips(half):
+            share = jnp.dot(gated[...], wout[:, columns], preferred_element_type=jnp.float32)
+            psend[dz] = share.astype(jnp.bfloat16)
+            p_copies[dz] = send(psend.at[dz], precv.at[dz], p_send.at[dz], p_recv.at[dz], chan=partner)
+
+    def for_chips():
         for dz in order:
-            share = jnp.dot(gated[half], wout[:, lanes_of(chan_of(dz))], preferred_element_type=jnp.float32)
-            p_copies[half, dz].wait_recv()
-            share = share + precv[half, dz].astype(jnp.float32)
+            share = jnp.dot(gated[...], wout[:, lanes_of(chan_of(dz))], preferred_element_type=jnp.float32)
+            p_copies[dz].wait_recv()
+            share = share + precv[dz].astype(jnp.float32)
             if dz:
-                ssend[half, dz - 1] = share.astype(jnp.bfloat16)
-                s_copies[half, dz] = send(
-                    ssend.at[half, dz - 1],
-                    srecv.at[half, dz - 1],
-                    s_send.at[half, dz - 1],
-                    s_recv.at[half, dz - 1],
-                    chan=chan_of(dz),
+                ssend[dz - 1] = share.astype(jnp.bfloat16)
+                s_copies[dz] = send(
+                    ssend.at[dz - 1], srecv.at[dz - 1], s_send.at[dz - 1], s_recv.at[dz - 1], chan=chan_of(dz)
                 )
             else:
-                share_own[half] = share
-
-    def add_up(half):
-        total = share_own[half]
-        for dz in range(1, n_z):
-            s_copies[half, dz].wait_recv()
-            total = total + srecv[half, dz - 1].astype(jnp.float32)
-        return total
-
-    keys_values(0)
-    queries(0)
+                share_own[...] = share
+
+    keys_values()
     unpack_filters()
     lax.fori_loop(0, groups, own_early, 0)
-    keys_values(1)
+    lax.fori_loop(0, groups, own_late, 0)
+    queries()
     for ds in range(1, n_seq):
         other_early(ds)
-    wout_copy.wait()
-    for_partner(0)
-    queries(1)
-    lax.fori_loop(0, groups, own_late, 0)
-    for_chips(0)
     for ds in range(1, n_seq):
         other_late(ds)
-    for_partner(1)
-    for_chips(1)
-    lead = add_up(0)
-    tail = add_up(1)
+    wout_copy.wait()
+    for_partner()
+    for_chips()
+    total = share_own[...]
+    for dz in range(1, n_z):
+        s_copies[dz].wait_recv()
+        total = total + srecv[dz - 1].astype(jnp.float32)
+    lead = total[:seg]
+    tail = total[seg:]
     keep = in_order((seg, chans))
     out_ref[0:seg, :] = jnp.where(keep, lead, tail).astype(jnp.bfloat16)
     out_ref[seg:rows, :] = jnp.where(keep, tail, lead).astype(jnp.bfloat16)
@@ -372,38 +354,38 @@
         scratch_shapes=[
             pltpu.SMEM(block_table.shape, jnp.int32),
             pltpu.VMEM((rows, chans), bf16),
-            pltpu.VMEM((2, seg, chans), bf16),
-            pltpu.VMEM((2, n_z, seg, 2 * chans), bf16),
+            pltpu.VMEM((rows, chans), bf16),
+            pltpu.VMEM((n_z, rows, 2 * chans), bf16),
             pltpu.VMEM((n_seq, rows, chans), bf16),
             pltpu.VMEM((3, width, chans), bf16),
             pltpu.VMEM((chans, width), bf16),
-            pltpu.VMEM((2, 3, seg, chans), f32),
+            pltpu.VMEM((3, rows, chans), f32),
             pltpu.VMEM((groups, 2 * seg + n_seq * rows, LANES), f32),
             pltpu.VMEM((2, seg, chans), bf16),
             pltpu.VMEM((2, n_seq - 1, seg, chans), bf16),
             pltpu.VMEM((n_seq + 1, groups, seg, LANES), f32),
             pltpu.VMEM((2, groups, seg, LANES), f32),
-            pltpu.VMEM((2, seg, chans), bf16),
-            pltpu.VMEM((2, n_z, seg, chans), bf16),
-            pltpu.VMEM((2, n_z, seg, chans), bf16),
-            pltpu.VMEM((2, n_z - 1, seg, chans), bf16),
-            pltpu.VMEM((2, n_z - 1, seg, chans), bf16),
-            pltpu.VMEM((2, seg, chans), f32),
+            pltpu.VMEM((rows, chans), bf16),
+            pltpu.VMEM((n_z, rows, chans), bf16),
+            pltpu.VMEM((n_z, rows, chans), bf16),
+            pltpu.VMEM((n_z - 1, rows, chans), bf16),
+            pltpu.VMEM((n_z - 1, rows, chans), bf16),
+            pltpu.VMEM((rows, chans), f32),
             dma((3,)),
+            dma((2, n_z)),
+            dma,
+            dma((n_z - 1,)),
+            dma((n_z - 1,)),
             dma((n_z,)),
-            dma,
-            dma((2, n_z - 1)),
-            dma((2, n_z - 1)),
-            dma((2, n_z)),
-            dma((2, n_z)),
+            dma((n_z,)),
             dma((n_seq - 1,)),
             dma((n_seq - 1,)),
             dma((2, n_seq - 1)),
             dma((2, n_seq - 1)),
-            dma((2, n_z)),
-            dma((2, n_z)),
-            dma((2, n_z - 1)),
-            dma((2, n_z - 1)),
+            dma((n_z,)),
+            dma((n_z,)),
+            dma((n_z - 1,)),
+            dma((n_z - 1,)),
         ],
         compiler_params=pltpu.CompilerParams(
             collective_id=0, has_side_effects=True, vmem_limit_bytes=64 * 1024 * 1024

time: 34.2 us -> 32.6 us (0.953)
  Pallas kernels: 32.5 us -> 30.9 us
    pallas_call x1, Pallas kernels: 32.5 us -> 30.9 us  [on_device(): pl.pallas_call(functools.partial(kernel, n_seq, n_chan), out_shape=jax.Sh...]
where the time goes in v4:
time: 32.6 us; the launch traced here: 32.4 us
  Pallas kernels  30.9 us (95%)
  local copies, waits for them, and re-layouts  1.47 us (5%)
    pallas_call x1, Pallas kernels, on_device(): pl.pallas_call(functools.partial(kernel, n_seq, n_chan), out_shape=jax.Sh...  30.9 us
    unnamed x1, local copies, waits for them, and re-layouts  1.47 us

profile of v4, /device:TPU:0, one launch (start us, length us, event | category | flops | bytes accessed | tf_op | source)
XLA Modules:
  0.0 32.4 jit_solution(4388167785855927424)
XLA Ops:
  0.0 30.9 %shard_map.55 = bf16[64,512]{1,0:T(8,128)(2,1)} custom-call(bf16[64,512]{1,0:T(8,128)(2,1)} %hidden_ref.1, bf16[64,512]{1,0:T(8,128)(2,1)} %filters_ref.1, bf16[3,4096,512]{2,1,0:T(8,128)(2,1)} %win_ref.1, bf16[512,4096]{1,0:T(8,128)(2,1)} %wout_ref.1, s32[8]{0:T(128)} %table_hbm.1), custom_call_target="tpu_custom_call" | custom-call | flops 1073741824 | bytes 16777216 | tf_op jit(solution)/shard_map/pallas_call | solution.py:349
  30.9 1.5 %copy.7 = bf16[64,512]{1,0:T(8,128)(2,1)} copy(bf16[64,512]{1,0:T(8,128)(2,1)} %shard_map.55) | data formatting | bytes 131072

commit v5 on v4

--- a/solution.py
+++ b/solution.py
@@ -30,8 +30,6 @@
     table_hbm,
     out_ref,
     table_ref,
-    held,
-    ordered,
     hbuf,
     fbuf,
     win,
@@ -97,7 +95,7 @@
         return copy
 
     own_table = pltpu.make_async_copy(table_hbm, table_ref, own_sem.at[0])
-    own_hidden = pltpu.make_async_copy(hidden_ref, held, own_sem.at[1])
+    own_hidden = pltpu.make_async_copy(hidden_ref, hbuf.at[z, :, lanes_of(core)], own_sem.at[1])
     own_filters = pltpu.make_async_copy(filters_ref, fbuf.at[seq], own_sem.at[2])
     own_table.start()
     own_hidden.start()
@@ -123,31 +121,14 @@
     own_filters.start()
     wout_copy = pltpu.make_async_copy(wout_ref, wout, wout_sem)
 
-    own_table.wait()
-    first = table_ref[2 * seq]
-    second = table_ref[2 * seq + 1]
-    early = jnp.minimum(first, second)
-
-    def in_order(shape):
-        return jnp.full(shape, first) < jnp.full(shape, second)
-
-    own_hidden.wait()
-    for group in range(groups):
-        lanes = slice(group * LANES, (group + 1) * LANES)
-        top = held[0:seg, lanes].astype(jnp.float32)
-        bottom = held[seg:rows, lanes].astype(jnp.float32)
-        keep = in_order((seg, LANES))
-        ordered[0:seg, lanes] = jnp.where(keep, top, bottom).astype(jnp.bfloat16)
-        ordered[seg:rows, lanes] = jnp.where(keep, bottom, top).astype(jnp.bfloat16)
-    hbuf[z, :, lanes_of(core)] = ordered[...]
     pl.semaphore_wait(barrier, n_seq - 1 + n_z)
 
     to_chip, to_partner = {}, {}
     for dz in range(n_z - 1, 0, -1):
         to_chip[dz] = send(
-            ordered, hbuf.at[z, :, lanes_of(core)], hz_send.at[dz - 1], hz_recv.at[dz - 1], chan=chan_of(dz)
+            hidden_ref, hbuf.at[z, :, lanes_of(core)], hz_send.at[dz - 1], hz_recv.at[dz - 1], chan=chan_of(dz)
         )
-    to_partner[0] = send(ordered, hbuf.at[z, :, lanes_of(core)], hp_send.at[0], hp_recv.at[0], chan=partner)
+    to_partner[0] = send(hidden_ref, hbuf.at[z, :, lanes_of(core)], hp_send.at[0], hp_recv.at[0], chan=partner)
     filter_copies = [
         send(filters_ref, fbuf.at[seq], f_send.at[ds - 1], f_recv.at[ds - 1], seq=flip(seq, ds))
         for ds in range(1, n_seq)
@@ -165,6 +146,7 @@
     m_copies = {}
 
     def keys_values():
+        own_hidden.wait()
         for dz in range(n_z):
             if dz:
                 to_chip[dz].wait_recv()
@@ -179,11 +161,17 @@
                     copy.start()
             if dz == min(1, n_z - 1):
                 wout_copy.start()
+
+    def exchange():
         for half in range(2):
-            part = slice(half * seg, (half + 1) * seg)
             for group in range(groups):
                 lanes = slice(group * LANES, (group + 1) * LANES)
-                product = streams[1, part, lanes] * streams[2, part, lanes]
+                product = streams[1, :, lanes] * streams[2, :, lanes]
+                keep = in_order((seg, LANES))
+                if half == 0:
+                    product = jnp.where(keep, product[:seg], product[seg:])
+                else:
+                    product = jnp.where(keep, product[seg:], product[:seg])
                 mwork[half, group] = product
                 msend[half, :, lanes] = product.astype(jnp.bfloat16)
             for ds in range(1, n_seq):
@@ -237,7 +225,6 @@
             acc[half, group, 8 * a : 8 * a + 8, :] = totals[a]
 
     count = 2 * n_seq
-    zero = early * 0
 
     def own_early(group, carry):
         (lead,) = convolve([(zero, zeros())], group, 0, lower=True)
@@ -288,11 +275,15 @@
     p_copies, s_copies = {}, {}
 
     def for_partner():
-        for half in range(2):
-            part = slice(half * seg, (half + 1) * seg)
-            for group in range(groups):
-                lanes = slice(group * LANES, (group + 1) * LANES)
-                gated[part, lanes] = (streams[0, part, lanes] * acc[half, group]).astype(jnp.bfloat16)
+        for group in range(groups):
+            lanes = slice(group * LANES, (group + 1) * LANES)
+            keep = in_order((seg, LANES))
+            lead = acc[0, group]
+            tail = acc[1, group]
+            top = streams[0, 0:seg, lanes] * jnp.where(keep, lead, tail)
+            bottom = streams[0, seg:rows, lanes] * jnp.where(keep, tail, lead)
+            gated[0:seg, lanes] = top.astype(jnp.bfloat16)
+            gated[seg:rows, lanes] = bottom.astype(jnp.bfloat16)
         for dz in order:
             columns = lanes_of(2 * flip(z, dz) + 1 - core)
             share = jnp.dot(gated[...], wout[:, columns], preferred_element_type=jnp.float32)
@@ -313,6 +304,16 @@
                 share_own[...] = share
 
     keys_values()
+    own_table.wait()
+    first = table_ref[2 * seq]
+    second = table_ref[2 * seq + 1]
+    early = jnp.minimum(first, second)
+    zero = early * 0
+
+    def in_order(shape):
+        return jnp.full(shape, first) < jnp.full(shape, second)
+
+    exchange()
     unpack_filters()
     lax.fori_loop(0, groups, own_early, 0)
     lax.fori_loop(0, groups, own_late, 0)
@@ -328,11 +329,7 @@
     for dz in range(1, n_z):
         s_copies[dz].wait_recv()
         total = total + srecv[dz - 1].astype(jnp.float32)
-    lead = total[:seg]
-    tail = total[seg:]
-    keep = in_order((seg, chans))
-    out_ref[0:seg, :] = jnp.where(keep, lead, tail).astype(jnp.bfloat16)
-    out_ref[seg:rows, :] = jnp.where(keep, tail, lead).astype(jnp.bfloat16)
+    out_ref[...] = total.astype(jnp.bfloat16)
     for copy in pending:
         copy.wait_send()
 
@@ -353,8 +350,6 @@
         out_specs=pl.BlockSpec(memory_space=pltpu.VMEM),
         scratch_shapes=[
             pltpu.SMEM(block_table.shape, jnp.int32),
-            pltpu.VMEM((rows, chans), bf16),
-            pltpu.VMEM((rows, chans), bf16),
             pltpu.VMEM((n_z, rows, 2 * chans), bf16),
             pltpu.VMEM((n_seq, rows, chans), bf16),
             pltpu.VMEM((3, width, chans), bf16),

time: 32.6 us -> 32.9 us (level)
  no operation moved by 1% of the time
where the time goes in v5:
time: 32.9 us; the launch traced here: 32.7 us
  Pallas kernels  31.2 us (95%)
  local copies, waits for them, and re-layouts  1.47 us (4%)
    pallas_call x1, Pallas kernels, on_device(): pl.pallas_call(functools.partial(kernel, n_seq, n_chan), out_shape=jax.Sh...  31.2 us
    unnamed x1, local copies, waits for them, and re-layouts  1.47 us

profile of v5, /device:TPU:0, one launch (start us, length us, event | category | flops | bytes accessed | tf_op | source)
XLA Modules:
  0.0 32.7 jit_solution(5659113653979570378)
XLA Ops:
  0.0 31.2 %shard_map.55 = bf16[64,512]{1,0:T(8,128)(2,1)} custom-call(bf16[64,512]{1,0:T(8,128)(2,1)} %hidden_ref.1, bf16[64,512]{1,0:T(8,128)(2,1)} %filters_ref.1, bf16[3,4096,512]{2,1,0:T(8,128)(2,1)} %win_ref.1, bf16[512,4096]{1,0:T(8,128)(2,1)} %wout_ref.1, s32[8]{0:T(128)} %table_hbm.1), custom_call_target="tpu_custom_call" | custom-call | flops 1073741824 | bytes 16777216 | tf_op jit(solution)/shard_map/pallas_call | solution.py:346
  31.3 1.5 %copy.7 = bf16[64,512]{1,0:T(8,128)(2,1)} copy(bf16[64,512]{1,0:T(8,128)(2,1)} %shard_map.55) | data formatting | bytes 131072

commit v6 on v5

--- a/solution.py
+++ b/solution.py
@@ -124,7 +124,7 @@
     pl.semaphore_wait(barrier, n_seq - 1 + n_z)
 
     to_chip, to_partner = {}, {}
-    for dz in range(n_z - 1, 0, -1):
+    for dz in range(1, n_z):
         to_chip[dz] = send(
             hidden_ref, hbuf.at[z, :, lanes_of(core)], hz_send.at[dz - 1], hz_recv.at[dz - 1], chan=chan_of(dz)
         )
@@ -134,14 +134,14 @@
         for ds in range(1, n_seq)
     ]
 
-    def project(dz, which):
+    def project(dz, which, columns, add=True):
         chip = flip(z, dz)
-        part = pl.ds(pl.multiple_of(chip * 2 * chans, 2 * chans), 2 * chans)
-        total = jnp.dot(hbuf[chip], win[which, part, :], preferred_element_type=jnp.float32)
-        if dz == 0:
-            streams[which] = total
-        else:
-            streams[which] += total
+        start = chip * 2 * chans + columns.start
+        part = pl.ds(pl.multiple_of(start, chans), columns.size)
+        total = jnp.dot(hbuf[chip, :, columns], win[which, part, :], preferred_element_type=jnp.float32)
+        if add:
+            total = streams[which] + total
+        streams[which] = total
 
     m_copies = {}
 
@@ -152,10 +152,12 @@
                 to_chip[dz].wait_recv()
                 spot = hbuf.at[flip(z, dz), :, lanes_of(core)]
                 to_partner[dz] = send(spot, spot, hp_send.at[dz], hp_recv.at[dz], chan=partner)
+            kv_copies[dz].wait()
+            project(dz, 1, lanes_of(core), dz > 0)
+            project(dz, 2, lanes_of(core), dz > 0)
             to_partner[dz].wait_recv()
-            kv_copies[dz].wait()
-            project(dz, 1)
-            project(dz, 2)
+            project(dz, 1, lanes_of(1 - core))
+            project(dz, 2, lanes_of(1 - core))
             if dz == 0:
                 for copy in q_copies:
                     copy.start()
@@ -186,7 +188,7 @@
     def queries():
         for dz in range(n_z):
             q_copies[dz].wait()
-            project(dz, 0)
+            project(dz, 0, pl.ds(0, 2 * chans), dz > 0)
 
     def unpack_filters():
         own_filters.wait()

time: 32.9 us -> 32 us (0.973)
  Pallas kernels: 31.2 us -> 30.4 us
    pallas_call x1, Pallas kernels: 31.2 us -> 30.4 us  [on_device(): pl.pallas_call(functools.partial(kernel, n_seq, n_chan), out_shape=jax.Sh...]
where the time goes in v6:
time: 32 us; the launch traced here: 31.9 us
  Pallas kernels  30.4 us (95%)
  local copies, waits for them, and re-layouts  1.47 us (5%)
    pallas_call x1, Pallas kernels, on_device(): pl.pallas_call(functools.partial(kernel, n_seq, n_chan), out_shape=jax.Sh...  30.4 us
    unnamed x1, local copies, waits for them, and re-layouts  1.47 us

profile of v6, /device:TPU:0, one launch (start us, length us, event | category | flops | bytes accessed | tf_op | source)
XLA Modules:
  0.0 31.9 jit_solution(17290274639591934776)
XLA Ops:
  0.0 30.4 %shard_map.55 = bf16[64,512]{1,0:T(8,128)(2,1)} custom-call(bf16[64,512]{1,0:T(8,128)(2,1)} %hidden_ref.1, bf16[64,512]{1,0:T(8,128)(2,1)} %filters_ref.1, bf16[3,4096,512]{2,1,0:T(8,128)(2,1)} %win_ref.1, bf16[512,4096]{1,0:T(8,128)(2,1)} %wout_ref.1, s32[8]{0:T(128)} %table_hbm.1), custom_call_target="tpu_custom_call" | custom-call | flops 1073741824 | bytes 16777216 | tf_op jit(solution)/shard_map/pallas_call | solution.py:348
  30.4 1.5 %copy.7 = bf16[64,512]{1,0:T(8,128)(2,1)} copy(bf16[64,512]{1,0:T(8,128)(2,1)} %shard_map.55) | data formatting | bytes 131072

commit v7 on v6

--- a/solution.py
+++ b/solution.py
@@ -275,6 +275,10 @@
 
     order = list(range(n_z - 1, -1, -1))
     p_copies, s_copies = {}, {}
+    relay = n_z == 4
+    at_end = 1 - ((z + 1) // 2) % 2
+    if relay:
+        order = [3, 1, 2, 0]
 
     def for_partner():
         for group in range(groups):
@@ -297,13 +301,41 @@
             share = jnp.dot(gated[...], wout[:, lanes_of(chan_of(dz))], preferred_element_type=jnp.float32)
             p_copies[dz].wait_recv()
             share = share + precv[dz].astype(jnp.float32)
-            if dz:
+            if dz == 0:
+                share_own[...] = share
+                continue
+            target, slot = chan_of(dz), dz - 1
+            if relay and dz == 3:
+                target = 2 * ((1 - at_end) * flip(z, 3) + at_end * flip(z, 1)) + core
+                slot = 2 + at_end
+            if relay and dz == 2:
+
+                @pl.when(at_end == 0)
+                def _():
+                    relayed().wait_recv()
+                    ssend[1] = (share + srecv[3].astype(jnp.float32)).astype(jnp.bfloat16)
+
+                @pl.when(at_end == 1)
+                def _():
+                    ssend[1] = share.astype(jnp.bfloat16)
+            else:
                 ssend[dz - 1] = share.astype(jnp.bfloat16)
-                s_copies[dz] = send(
-                    ssend.at[dz - 1], srecv.at[dz - 1], s_send.at[dz - 1], s_recv.at[dz - 1], chan=chan_of(dz)
-                )
-            else:
-                share_own[...] = share
+            s_copies[dz] = send(
+                ssend.at[dz - 1], srecv.at[slot], s_send.at[dz - 1], s_recv.at[slot], chan=target
+            )
+
+    def landing(slot):
+        return pltpu.make_async_remote_copy(
+            src_ref=ssend.at[0],
+            dst_ref=srecv.at[slot],
+            send_sem=s_send.at[0],
+            recv_sem=s_recv.at[slot],
+            device_id={"chan": partner},
+            device_id_type=MESH,
+        )
+
+    def relayed():
+        return landing(3)
 
     keys_values()
     own_table.wait()
@@ -327,9 +359,16 @@
     wout_copy.wait()
     for_partner()
     for_chips()
+    if relay:
+
+        @pl.when(at_end == 0)
+        def _():
+            landing(2).wait_recv()
+            share_own[...] += srecv[2].astype(jnp.float32)
+
     total = share_own[...]
-    for dz in range(1, n_z):
-        s_copies[dz].wait_recv()
+    for dz in range(1, 3 if relay else n_z):
+        landing(dz - 1).wait_recv()
         total = total + srecv[dz - 1].astype(jnp.float32)
     out_ref[...] = total.astype(jnp.bfloat16)
     for copy in pending:
@@ -366,7 +405,7 @@
             pltpu.VMEM((n_z, rows, chans), bf16),
             pltpu.VMEM((n_z, rows, chans), bf16),
             pltpu.VMEM((n_z - 1, rows, chans), bf16),
-            pltpu.VMEM((n_z - 1, rows, chans), bf16),
+            pltpu.VMEM((n_z, rows, chans), bf16),
             pltpu.VMEM((rows, chans), f32),
             dma((3,)),
             dma((2, n_z)),
@@ -382,7 +421,7 @@
             dma((n_z,)),
             dma((n_z,)),
             dma((n_z - 1,)),
-            dma((n_z - 1,)),
+            dma((n_z,)),
         ],
         compiler_params=pltpu.CompilerParams(
             collective_id=0, has_side_effects=True, vmem_limit_bytes=64 * 1024 * 1024

time: 32 us -> 31.8 us (level)
  no operation moved by 1% of the time
where the time goes in v7:
time: 31.8 us; the launch traced here: 31.6 us
  Pallas kernels  30.2 us (95%)
  local copies, waits for them, and re-layouts  1.47 us (5%)
    pallas_call x1, Pallas kernels, on_device(): pl.pallas_call(functools.partial(kernel, n_seq, n_chan), out_shape=jax.Sh...  30.2 us
    unnamed x1, local copies, waits for them, and re-layouts  1.47 us

profile of v7, /device:TPU:0, one launch (start us, length us, event | category | flops | bytes accessed | tf_op | source)
XLA Modules:
  0.0 31.6 jit_solution(17181010720186040110)
XLA Ops:
  0.0 30.2 %shard_map.55 = bf16[64,512]{1,0:T(8,128)(2,1)} custom-call(bf16[64,512]{1,0:T(8,128)(2,1)} %hidden_ref.1, bf16[64,512]{1,0:T(8,128)(2,1)} %filters_ref.1, bf16[3,4096,512]{2,1,0:T(8,128)(2,1)} %win_ref.1, bf16[512,4096]{1,0:T(8,128)(2,1)} %wout_ref.1, s32[8]{0:T(128)} %table_hbm.1), custom_call_target="tpu_custom_call" | custom-call | flops 1073741824 | bytes 16777216 | tf_op jit(solution)/shard_map/pallas_call | solution.py:387
  30.2 1.5 %copy.7 = bf16[64,512]{1,0:T(8,128)(2,1)} copy(bf16[64,512]{1,0:T(8,128)(2,1)} %shard_map.55) | data formatting | bytes 131072

commit v8 on v7

--- a/solution.py
+++ b/solution.py
@@ -148,6 +148,8 @@
     def keys_values():
         own_hidden.wait()
         for dz in range(n_z):
+            if dz == n_z - 1:
+                unpack_filters()
             if dz:
                 to_chip[dz].wait_recv()
                 spot = hbuf.at[flip(z, dz), :, lanes_of(core)]
@@ -187,7 +189,6 @@
 
     def queries():
         for dz in range(n_z):
-            q_copies[dz].wait()
             project(dz, 0, pl.ds(0, 2 * chans), dz > 0)
 
     def unpack_filters():
@@ -226,6 +227,10 @@
         for a in range(tiles):
             acc[half, group, 8 * a : 8 * a + 8, :] = totals[a]
 
+    def for_groups(body):
+        for group in range(groups):
+            body(group, 0)
+
     count = 2 * n_seq
 
     def own_early(group, carry):
@@ -261,7 +266,7 @@
             store_acc(1, group, tail)
             return carry
 
-        lax.fori_loop(0, groups, body, 0)
+        for_groups(body)
 
     def other_late(ds):
         theirs = receive(1, ds)
@@ -271,7 +276,7 @@
             store_acc(1, group, tail)
             return carry
 
-        lax.fori_loop(0, groups, body, 0)
+        for_groups(body)
 
     order = list(range(n_z - 1, -1, -1))
     p_copies, s_copies = {}, {}
@@ -348,10 +353,11 @@
         return jnp.full(shape, first) < jnp.full(shape, second)
 
     exchange()
-    unpack_filters()
-    lax.fori_loop(0, groups, own_early, 0)
-    lax.fori_loop(0, groups, own_late, 0)
+    for copy in q_copies:
+        copy.wait()
+    for_groups(own_early)
     queries()
+    for_groups(own_late)
     for ds in range(1, n_seq):
         other_early(ds)
     for ds in range(1, n_seq):

time: 31.8 us -> 31.7 us (level)
  no operation moved by 1% of the time
where the time goes in v8:
time: 31.7 us; the launch traced here: 31.6 us
  Pallas kernels  30.1 us (95%)
  local copies, waits for them, and re-layouts  1.47 us (5%)
    pallas_call x1, Pallas kernels, on_device(): pl.pallas_call(functools.partial(kernel, n_seq, n_chan), out_shape=jax.Sh...  30.1 us
    unnamed x1, local copies, waits for them, and re-layouts  1.47 us

profile of v8, /device:TPU:0, one launch (start us, length us, event | category | flops | bytes accessed | tf_op | source)
XLA Modules:
  0.0 31.6 jit_solution(11465359263208370251)
XLA Ops:
  0.0 30.1 %shard_map.55 = bf16[64,512]{1,0:T(8,128)(2,1)} custom-call(bf16[64,512]{1,0:T(8,128)(2,1)} %hidden_ref.1, bf16[64,512]{1,0:T(8,128)(2,1)} %filters_ref.1, bf16[3,4096,512]{2,1,0:T(8,128)(2,1)} %win_ref.1, bf16[512,4096]{1,0:T(8,128)(2,1)} %wout_ref.1, s32[8]{0:T(128)} %table_hbm.1), custom_call_target="tpu_custom_call" | custom-call | flops 1073741824 | bytes 16777216 | tf_op jit(solution)/shard_map/pallas_call | solution.py:393
  30.1 1.5 %copy.7 = bf16[64,512]{1,0:T(8,128)(2,1)} copy(bf16[64,512]{1,0:T(8,128)(2,1)} %shard_map.55) | data formatting | bytes 131072
